TPU v7x, 1024 devices: a whole 4x8x16 slice. The times are simulated.
1024 devices in a mesh: seq: 64 (over y_hi, z, core), batch: 16 (over x, y_lo).
Axes of the slice: x: 4, y: 8 (y_hi: 2, y_lo: 4; y = y_hi * 4 + y_lo), z: 16, core: 2. Of those that a mesh axis runs over, the one named last changes fastest.
Arguments:
- queries: bfloat16 [32, 512, 64, 128], P('batch', 'seq'), parts along dimension 0, may hold values from -5 to 5
- grad_out: bfloat16 [32, 512, 64, 128], P('batch', 'seq'), parts along dimension 0, may hold values from -6 to 6
- keys: bfloat16 [16384, 64, 128], P('batch', 'seq'), parts along dimension 0, may hold values from -5 to 5
- values: bfloat16 [16384, 64, 128], P('batch', 'seq'), parts along dimension 0, may hold values from -6 to 6
- block_offsets: int32 [48], P('batch'), parts along dimension 0, may hold values from 261120 to 261632, as said below
Outputs:
- grad_queries: bfloat16 [32, 512, 64, 128], P('batch', 'seq'), parts along dimension 0
- grad_keys: bfloat16 [16384, 64, 128], P(('batch', 'seq')), parts along dimension 0
- grad_values: bfloat16 [16384, 64, 128], P(('batch', 'seq')), parts along dimension 0
There are 16 independent parts, one for each index of `batch`. A program takes and returns all parts, laid end to end along the dimension named above; each array names one. Nothing has to cross between parts.
Inputs may be any that keep to these rules, and one draw needn't show every extreme that they name: block_offsets[0] is 261120; each query block starts 0 to 512 positions after the key block's start, and some query block starts exactly 512 after it.
All inputs are finite; a program needn't handle non-finite values.
Results may differ from a plain program's by a relative error of at most 0.012.
The roundings to bfloat16 on the way count: a program that leaves them out, or rounds other values in their place, can miss the bound.
Values may be sent and summed in bfloat16 or wider, within the bound.
A program may use at most 32 MiB of HBM per device.

v0:
```python
import jax
import jax.numpy as jnp
from jax import lax
from jax.sharding import PartitionSpec as P


def block_backward(q_head, grad_head, keys, values, query_pos, key_pos):
    score_scale = keys.shape[-1] ** (-0.5)
    scores = (
        jnp.einsum("qhd,khd->hqk", q_head, keys, preferred_element_type=jnp.float32) * score_scale
    )
    visible = key_pos[None, :] <= query_pos[:, None]
    scores = jnp.where(visible[None], scores, -jnp.inf)
    row_max = jnp.max(scores, axis=-1, keepdims=True)
    expo = jnp.exp(scores - row_max)
    attend = expo / jnp.sum(expo, axis=-1, keepdims=True)
    attend_b = attend.astype(jnp.bfloat16)
    outputs = jnp.einsum("hqk,khd->qhd", attend_b, values, preferred_element_type=jnp.float32)
    row_delta = jnp.sum(grad_head.astype(jnp.float32) * outputs, axis=-1)
    grad_attend = jnp.einsum("qhd,khd->hqk", grad_head, values, preferred_element_type=jnp.float32)
    grad_scores = (attend * (grad_attend - jnp.transpose(row_delta)[:, :, None])).astype(
        jnp.bfloat16
    )
    grad_q = (
        jnp.einsum("hqk,khd->qhd", grad_scores, keys, preferred_element_type=jnp.float32)
        * score_scale
    ).astype(jnp.bfloat16)
    grad_k = (
        jnp.einsum("hqk,qhd->khd", grad_scores, q_head, preferred_element_type=jnp.float32)
        * score_scale
    )
    grad_v = jnp.einsum("hqk,qhd->khd", attend_b, grad_head, preferred_element_type=jnp.float32)
    return (grad_q, grad_k, grad_v)


def body(queries, grad_out, keys, values, block_offsets):
    devices = lax.axis_size("seq")
    num_blocks = queries.shape[0]
    tok_rows = queries.shape[1]
    query_len = tok_rows * devices
    key_len = keys.shape[0]
    key_pos = block_offsets[0] + jnp.arange(key_len, dtype=jnp.int32)
    query_pos = block_offsets[1:][:, None] + jnp.arange(query_len, dtype=jnp.int32)[None, :]
    grad_k_sum = jnp.zeros(keys.shape, jnp.float32)
    grad_v_sum = jnp.zeros(keys.shape, jnp.float32)
    returned = []
    pending = None
    for block in range(num_blocks):
        q_head, g_head = (
            lax.all_to_all(queries[block], "seq", split_axis=1, concat_axis=0, tiled=True),
            lax.all_to_all(grad_out[block], "seq", split_axis=1, concat_axis=0, tiled=True),
        )
        grad_q, grad_k, grad_v = block_backward(
            q_head, g_head, keys, values, query_pos[block], key_pos
        )
        grad_k_sum = grad_k_sum + grad_k
        grad_v_sum = grad_v_sum + grad_v
        if block + 1 < num_blocks:
            returned.append(
                lax.all_to_all(grad_q, "seq", split_axis=0, concat_axis=1, tiled=True)[None]
            )
        else:
            pending = grad_q[None]
    grad_k_b = grad_k_sum.astype(jnp.bfloat16)
    grad_v_b = grad_v_sum.astype(jnp.bfloat16)
    last_rows = lax.all_to_all(pending, "seq", split_axis=1, concat_axis=2, tiled=True)
    grad_keys, grad_values = (
        lax.all_to_all(grad_k_b, "seq", split_axis=0, concat_axis=1, tiled=True),
        lax.all_to_all(grad_v_b, "seq", split_axis=0, concat_axis=1, tiled=True),
    )
    grad_queries = jnp.concatenate(returned + [last_rows], axis=0)
    return (grad_queries, grad_keys, grad_values)


def solution(mesh):
    in_specs = (
        P("batch", "seq", None, None),
        P("batch", "seq", None, None),
        P("batch", "seq", None),
        P("batch", "seq", None),
        P("batch"),
    )
    out_specs = (
        P("batch", "seq", None, None),
        P(("batch", "seq"), None, None),
        P(("batch", "seq"), None, None),
    )
    return jax.shard_map(body, mesh=mesh, in_specs=in_specs, out_specs=out_specs, check_vma=False)
```

profile of v0, /device:TPU:1, one launch (start us, length us, event | category | flops | bytes accessed | tf_op | source)
XLA Modules:
  0.0 247.0 jit_solution(1203527453476512981)
XLA Ops:
  2.4 26.1 %all-to-all-start.3 = ((bf16[8,64,128]{2,0,1:T(8,128)(2,1)}), bf16[8,64,128]{2,0,1:T(8,128)(2,1)S(1)}, u32[]{:S(2)}, u32[]{:S(2)}) async-start(bf16[8,64,128]{2,0,1:T(8,128)(2,1)} %bitcast.157), calls=%async_computation.3 | async-start | bytes 262144 | tf_op jit(solution)/shard_map/all_to_all | solution.py:50
  32.6 17.0 %all-to-all-done.3 = bf16[8,64,128]{2,0,1:T(8,128)(2,1)S(1)} async-done(((bf16[8,64,128]{2,0,1:T(8,128)(2,1)}), bf16[8,64,128]{2,0,1:T(8,128)(2,1)S(1)}, u32[]{:S(2)}, u32[]{:S(2)}) %all-to-all-start.3) | async-done | bytes 131104 | tf_op jit(solution)/shard_map/all_to_all | solution.py:50
  49.6 4.4 %all-to-all-start.4 = ((bf16[8,64,128]{2,0,1:T(8,128)(2,1)}), bf16[8,64,128]{2,0,1:T(8,128)(2,1)S(1)}, u32[]{:S(2)}, u32[]{:S(2)}) async-start(bf16[8,64,128]{2,0,1:T(8,128)(2,1)} %bitcast.156), calls=%async_computation.4 | async-start | bytes 262144 | tf_op jit(solution)/shard_map/all_to_all | solution.py:51
  55.6 19.6 %all-to-all-done.4 = bf16[8,64,128]{2,0,1:T(8,128)(2,1)S(1)} async-done(((bf16[8,64,128]{2,0,1:T(8,128)(2,1)}), bf16[8,64,128]{2,0,1:T(8,128)(2,1)S(1)}, u32[]{:S(2)}, u32[]{:S(2)}) %all-to-all-start.4) | async-done | bytes 131104 | tf_op jit(solution)/shard_map/all_to_all | solution.py:51
  75.2 5.2 %all-to-all-start = ((bf16[8,64,128]{2,0,1:T(8,128)(2,1)}), bf16[8,64,128]{2,0,1:T(8,128)(2,1)}, u32[]{:S(2)}, u32[]{:S(2)}) async-start(bf16[8,64,128]{2,0,1:T(8,128)(2,1)} %bitcast.159), calls=%async_computation | async-start | bytes 262144 | tf_op jit(solution)/shard_map/all_to_all | solution.py:50
  81.1 1.4 multiply_convert_fusion
  84.4 3.0 %reduce.10 = bf16[512,128]{1,0:T(8,128)(2,1)} reduce(bf16[512,1,1,128]{3,2,1,0:T(2,128)(2,1)} %bitcast.166, bf16[]{:T(256)} %broadcast.66), dimensions={1,2}, to_apply=%bitcast.162.reduce_sub_computation | reduce | bytes 262146
  87.3 1.6 reshape.176
  88.9 12.5 %all-to-all-done = bf16[8,64,128]{2,0,1:T(8,128)(2,1)} async-done(((bf16[8,64,128]{2,0,1:T(8,128)(2,1)}), bf16[8,64,128]{2,0,1:T(8,128)(2,1)}, u32[]{:S(2)}, u32[]{:S(2)}) %all-to-all-start) | async-done | bytes 131104 | tf_op jit(solution)/shard_map/all_to_all | solution.py:50
  101.5 5.4 %all-to-all-start.1 = ((bf16[8,64,128]{2,0,1:T(8,128)(2,1)}), bf16[8,64,128]{2,0,1:T(8,128)(2,1)}, u32[]{:S(2)}, u32[]{:S(2)}) async-start(bf16[8,64,128]{2,0,1:T(8,128)(2,1)} %bitcast.168), calls=%async_computation.1 | async-start | bytes 262144 | tf_op jit(solution)/shard_map/all_to_all | solution.py:51
  106.8 1.4 fusion.43
  108.8 1.8 fusion
  110.6 17.2 %all-to-all-done.1 = bf16[8,64,128]{2,0,1:T(8,128)(2,1)} async-done(((bf16[8,64,128]{2,0,1:T(8,128)(2,1)}), bf16[8,64,128]{2,0,1:T(8,128)(2,1)}, u32[]{:S(2)}, u32[]{:S(2)}) %all-to-all-start.1) | async-done | bytes 131104 | tf_op jit(solution)/shard_map/all_to_all | solution.py:51
  127.8 5.2 %all-to-all-start.5 = ((bf16[64,2,512]{2,1,0:T(2,128)(2,1)}), bf16[64,2,512]{2,1,0:T(2,128)(2,1)}, u32[]{:S(2)}, u32[]{:S(2)}) async-start(bf16[64,2,512]{2,1,0:T(2,128)(2,1)} %reshape.176), calls=%async_computation.5 | async-start | bytes 262144 | tf_op jit(solution)/shard_map/all_to_all | solution.py:66
  133.0 1.6 bitcast_convert_fusion.1
  134.6 1.8 copy.40
  136.4 2.3 fusion.13
  142.2 2.2 reduce.11
  144.4 1.6 reshape.178
  146.0 8.0 %all-to-all-done.5 = bf16[64,2,512]{2,1,0:T(2,128)(2,1)} async-done(((bf16[64,2,512]{2,1,0:T(2,128)(2,1)}), bf16[64,2,512]{2,1,0:T(2,128)(2,1)}, u32[]{:S(2)}, u32[]{:S(2)}) %all-to-all-start.5) | async-done | bytes 131104 | tf_op jit(solution)/shard_map/all_to_all | solution.py:66
  154.0 10.1 %all-to-all-start.2 = ((bf16[64,2,512]{2,1,0:T(2,128)(2,1)}), bf16[64,2,512]{2,1,0:T(2,128)(2,1)}, u32[]{:S(2)}, u32[]{:S(2)}) async-start(bf16[64,2,512]{2,1,0:T(2,128)(2,1)} %reshape.178), calls=%async_computation.2 | async-start | bytes 262144 | tf_op jit(solution)/shard_map/all_to_all | solution.py:60
  164.1 1.7 fusion.36
  165.8 2.1 fusion.7
  167.9 1.7 reduce.12
  170.4 14.6 %all-to-all-done.2 = bf16[64,2,512]{2,1,0:T(2,128)(2,1)} async-done(((bf16[64,2,512]{2,1,0:T(2,128)(2,1)}), bf16[64,2,512]{2,1,0:T(2,128)(2,1)}, u32[]{:S(2)}, u32[]{:S(2)}) %all-to-all-start.2) | async-done | bytes 131104 | tf_op jit(solution)/shard_map/all_to_all | solution.py:60
  185.1 4.5 %all-to-all-start.6 = ((bf16[64,2,1024]{2,1,0:T(2,128)(2,1)}), bf16[64,2,1024]{2,1,0:T(2,128)(2,1)S(1)}, u32[]{:S(2)}, u32[]{:S(2)}) async-start(bf16[64,2,1024]{2,1,0:T(2,128)(2,1)} %reshape.180), calls=%async_computation.6 | async-start | bytes 524288 | tf_op jit(solution)/shard_map/all_to_all | solution.py:68
  189.5 2.1 fusion.19
  193.6 22.1 %all-to-all-done.6 = bf16[64,2,1024]{2,1,0:T(2,128)(2,1)S(1)} async-done(((bf16[64,2,1024]{2,1,0:T(2,128)(2,1)}), bf16[64,2,1024]{2,1,0:T(2,128)(2,1)S(1)}, u32[]{:S(2)}, u32[]{:S(2)}) %all-to-all-start.6) | async-done | bytes 262176 | tf_op jit(solution)/shard_map/all_to_all | solution.py:68
  215.8 4.2 %all-to-all-start.7 = ((bf16[64,2,1024]{2,1,0:T(2,128)(2,1)}), bf16[64,2,1024]{2,1,0:T(2,128)(2,1)S(1)}, u32[]{:S(2)}, u32[]{:S(2)}) async-start(bf16[64,2,1024]{2,1,0:T(2,128)(2,1)} %reshape.182), calls=%async_computation.7 | async-start | bytes 524288 | tf_op jit(solution)/shard_map/all_to_all | solution.py:69
  220.0 1.4 reshape.177
  221.4 1.4 reshape.179
  224.6 21.3 %all-to-all-done.7 = bf16[64,2,1024]{2,1,0:T(2,128)(2,1)S(1)} async-done(((bf16[64,2,1024]{2,1,0:T(2,128)(2,1)}), bf16[64,2,1024]{2,1,0:T(2,128)(2,1)S(1)}, u32[]{:S(2)}, u32[]{:S(2)}) %all-to-all-start.7) | async-done | bytes 262176 | tf_op jit(solution)/shard_map/all_to_all | solution.py:69
  (50 shorter events, 19.6 us)
Async XLA Ops:
  0.6 53.4 %copy-start = (bf16[1024,1,128]{2,0,1:T(8,128)(2,1)S(1)}, bf16[1024,1,128]{2,0,1:T(8,128)(2,1)}, u32[]{:S(2)}) copy-start(bf16[1024,1,128]{2,0,1:T(8,128)(2,1)} %param.7) | copy-start | bytes 786436
  0.6 31.8 %copy-start.6 = (s32[3]{0:T(128)S(1)}, s32[3]{0:T(128)}, u32[]{:S(2)}) copy-start(s32[3]{0:T(128)} %param.9) | copy-start | bytes 40
  2.4 47.1 %all-to-all-start.3 = ((bf16[8,64,128]{2,0,1:T(8,128)(2,1)}), bf16[8,64,128]{2,0,1:T(8,128)(2,1)S(1)}, u32[]{:S(2)}, u32[]{:S(2)}) async-start(bf16[8,64,128]{2,0,1:T(8,128)(2,1)} %bitcast.157), calls=%async_computation.3 | async-start | bytes 262144 | tf_op jit(solution)/shard_map/all_to_all | solution.py:50
  49.6 5.0 %copy-start.5 = (bf16[8,64,128]{2,0,1:T(8,128)(2,1)}, bf16[8,64,128]{2,0,1:T(8,128)(2,1)S(1)}, u32[]{:S(2)}) copy-start(bf16[8,64,128]{2,0,1:T(8,128)(2,1)S(1)} %all-to-all-done.3) | copy-start | bytes 393220
  49.6 25.6 %all-to-all-start.4 = ((bf16[8,64,128]{2,0,1:T(8,128)(2,1)}), bf16[8,64,128]{2,0,1:T(8,128)(2,1)S(1)}, u32[]{:S(2)}, u32[]{:S(2)}) async-start(bf16[8,64,128]{2,0,1:T(8,128)(2,1)} %bitcast.156), calls=%async_computation.4 | async-start | bytes 262144 | tf_op jit(solution)/shard_map/all_to_all | solution.py:51
  55.1 25.5 %copy-start.3 = (bf16[1024,1,128]{2,0,1:T(8,128)(2,1)S(1)}, bf16[1024,1,128]{2,0,1:T(8,128)(2,1)}, u32[]{:S(2)}) copy-start(bf16[1024,1,128]{2,0,1:T(8,128)(2,1)} %param.8) | copy-start | bytes 786436
  75.2 26.3 %all-to-all-start = ((bf16[8,64,128]{2,0,1:T(8,128)(2,1)}), bf16[8,64,128]{2,0,1:T(8,128)(2,1)}, u32[]{:S(2)}, u32[]{:S(2)}) async-start(bf16[8,64,128]{2,0,1:T(8,128)(2,1)} %bitcast.159), calls=%async_computation | async-start | bytes 262144 | tf_op jit(solution)/shard_map/all_to_all | solution.py:50
  101.5 26.3 %all-to-all-start.1 = ((bf16[8,64,128]{2,0,1:T(8,128)(2,1)}), bf16[8,64,128]{2,0,1:T(8,128)(2,1)}, u32[]{:S(2)}, u32[]{:S(2)}) async-start(bf16[8,64,128]{2,0,1:T(8,128)(2,1)} %bitcast.168), calls=%async_computation.1 | async-start | bytes 262144 | tf_op jit(solution)/shard_map/all_to_all | solution.py:51
  127.8 26.2 %all-to-all-start.5 = ((bf16[64,2,512]{2,1,0:T(2,128)(2,1)}), bf16[64,2,512]{2,1,0:T(2,128)(2,1)}, u32[]{:S(2)}, u32[]{:S(2)}) async-start(bf16[64,2,512]{2,1,0:T(2,128)(2,1)} %reshape.176), calls=%async_computation.5 | async-start | bytes 262144 | tf_op jit(solution)/shard_map/all_to_all | solution.py:66
  136.4 2.4 copy-start.1
  136.4 2.4 copy-start.4
  140.1 1.0 copy-start.2
  154.0 31.1 %all-to-all-start.2 = ((bf16[64,2,512]{2,1,0:T(2,128)(2,1)}), bf16[64,2,512]{2,1,0:T(2,128)(2,1)}, u32[]{:S(2)}, u32[]{:S(2)}) async-start(bf16[64,2,512]{2,1,0:T(2,128)(2,1)} %reshape.178), calls=%async_computation.2 | async-start | bytes 262144 | tf_op jit(solution)/shard_map/all_to_all | solution.py:60
  185.1 30.7 %all-to-all-start.6 = ((bf16[64,2,1024]{2,1,0:T(2,128)(2,1)}), bf16[64,2,1024]{2,1,0:T(2,128)(2,1)S(1)}, u32[]{:S(2)}, u32[]{:S(2)}) async-start(bf16[64,2,1024]{2,1,0:T(2,128)(2,1)} %reshape.180), calls=%async_computation.6 | async-start | bytes 524288 | tf_op jit(solution)/shard_map/all_to_all | solution.py:68
  215.8 30.2 %all-to-all-start.7 = ((bf16[64,2,1024]{2,1,0:T(2,128)(2,1)}), bf16[64,2,1024]{2,1,0:T(2,128)(2,1)S(1)}, u32[]{:S(2)}, u32[]{:S(2)}) async-start(bf16[64,2,1024]{2,1,0:T(2,128)(2,1)} %reshape.182), calls=%async_computation.7 | async-start | bytes 524288 | tf_op jit(solution)/shard_map/all_to_all | solution.py:69
where the time goes:
time: 248 us; the launch traced here: 247 us
  waiting for transfers between devices  132 us (53%)
  starting transfers between devices  65 us (26%)
  local copies, waits for them, and re-layouts  20.5 us (8%)
  matrix products  15.4 us (6%)
  other arithmetic  12.8 us (5%)
    all_to_all x2, waiting for transfers between devices, body(): lax.all_to_all(grad_out[block], 'seq', split_axis=1, concat_axis=0, tiled...  36.8 us
    all_to_all x2, starting transfers between devices, body(): lax.all_to_all(queries[block], 'seq', split_axis=1, concat_axis=0, tiled=...  31.3 us
    all_to_all x2, waiting for transfers between devices, body(): lax.all_to_all(queries[block], 'seq', split_axis=1, concat_axis=0, tiled=...  29.5 us
    all_to_all x1, waiting for transfers between devices, body(): lax.all_to_all(grad_k_b, 'seq', split_axis=0, concat_axis=1, tiled=True)  22.1 us
    all_to_all x1, waiting for transfers between devices, body(): lax.all_to_all(grad_v_b, 'seq', split_axis=0, concat_axis=1, tiled=True)  21.3 us
    unnamed x34, local copies, waits for them, and re-layouts  14.9 us
    all_to_all x1, waiting for transfers between devices, body(): lax.all_to_all(grad_q, 'seq', split_axis=0, concat_axis=1, tiled=True)[None]  14.6 us
    all_to_all x1, starting transfers between devices, body(): lax.all_to_all(grad_q, 'seq', split_axis=0, concat_axis=1, tiled=True)[None]  10.1 us
  transfers between devices with their start and end apart: 8, of which 8 were waited for; matrix products, arithmetic and copies ran while one was open for 18% of the time, Pallas kernels for 0%

commit v1 on v0

v1 whole, which is shorter than its diff:
```python
import functools
import math

import jax
import jax.numpy as jnp
from jax import lax
from jax.experimental import pallas as pl
from jax.experimental.pallas import tpu as pltpu
from jax.sharding import PartitionSpec as P

MESH = pl.DeviceIdType.MESH
GROUP = 16
STEPS = ((1, 1), (0, 1), (1, 0), (0, 0))


def nt_dot(a, b):
    return lax.dot_general(a, b, (((1,), (1,)), ((), ())), preferred_element_type=jnp.float32)


def swap(x):
    return jnp.transpose(x.astype(jnp.float32), (1, 0, 2)).astype(jnp.bfloat16)


def kernel(
    offs, q_hbm, g_hbm, k_hbm, v_hbm, gq_out, gk_out, gv_out,
    q_in, g_in, k_ref, v_ref, kt_ref,
    send_a, recv_a, send_q, recv_q, send_kv, recv_kv,
    s_ref, dp_ref, pb_ref, gk_acc, gv_acc,
    in_sem, send_sem, recv_a_sem, recv_q_sem, recv_kv_sem,
):
    devices = send_a.shape[0]
    toks = q_in.shape[0]
    half = toks // 2
    key_len, hd = k_ref.shape
    tile = 256
    tiles = key_len // tile
    rows = GROUP * toks
    scale = hd ** -0.5

    me = lax.axis_index("seq")
    group, pos = me // GROUP, me % GROUP
    gy, gh = group // 2, group % 2

    def group_of(dy, dh):
        return lax.rem(gy + dy, 2) * 2 + lax.rem(gh + dh, 2)

    loads = [
        pltpu.make_async_copy(src, dst, in_sem.at[i])
        for i, (src, dst) in enumerate(
            ((q_hbm, q_in), (g_hbm, g_in), (k_hbm, k_ref), (v_hbm, v_ref))
        )
    ]
    for load in loads:
        load.start()

    barrier = pltpu.get_barrier_semaphore()

    def greet(i, carry):
        pl.semaphore_signal(
            barrier, inc=1, device_id={"seq": lax.rem(me + i, devices)}, device_id_type=MESH
        )
        return carry

    lax.fori_loop(1, devices, greet, 0)
    loads[0].wait()
    loads[1].wait()

    def exchange(step, target, src, dst, s_sem, r_sem, own):
        def one(i, carry):
            other = lax.rem(pos + i, GROUP)
            dev = target * GROUP + other
            pltpu.make_async_remote_copy(
                src_ref=src(dev, other), dst_ref=dst, send_sem=s_sem, recv_sem=r_sem,
                device_id={"seq": dev}, device_id_type=MESH,
            ).start()
            return carry

        if own:
            pltpu.make_async_copy(src(me, pos), dst, r_sem).start()
        lax.fori_loop(1 if own else 0, GROUP, one, 0)

    for step, (dy, dh) in enumerate(STEPS):
        target = group_of(dy, dh)
        heads = pl.ds(pl.multiple_of(target * GROUP, GROUP), GROUP)
        send_a[heads, 0:toks, :] = swap(q_in[:, heads, :])
        send_a[heads, toks : 2 * toks, :] = swap(g_in[:, heads, :])
        if step == 0:
            pl.semaphore_wait(barrier, devices - 1)
        exchange(
            step, target, lambda dev, other: send_a.at[dev], recv_a.at[step, pos],
            send_sem.at[0], recv_a_sem.at[step], step == 3,
        )

    loads[2].wait()
    loads[3].wait()
    for t in range(tiles):
        span = pl.ds(t * tile, tile)
        kt_ref[:, span] = jnp.transpose(k_ref[span, :].astype(jnp.float32)).astype(jnp.bfloat16)
    gk_acc[...] = jnp.zeros_like(gk_acc)
    gv_acc[...] = jnp.zeros_like(gv_acc)

    lane = lax.broadcasted_iota(jnp.int32, (1, rows), 1)
    sub = lax.broadcasted_iota(jnp.int32, (tile, rows), 0)
    in_tok = lane % toks
    shift = jnp.where(in_tok >= half, offs[2], offs[1]) - offs[0]
    local_pos = shift + (lane // toks) * half + in_tok % half

    for step, (dy, dh) in enumerate(STEPS):
        source = group_of(dy, dh)
        pltpu.make_async_copy(recv_a.at[step], recv_a.at[step], recv_a_sem.at[step]).wait()
        q = recv_a[step, :, 0:toks, :].reshape(rows, hd)
        g = recv_a[step, :, toks : 2 * toks, :].reshape(rows, hd)
        limit = local_pos + source * (GROUP * half)
        top = jnp.full((1, rows), -jnp.inf, jnp.float32)
        for t in range(tiles):
            span = pl.ds(t * tile, tile)
            s = nt_dot(k_ref[span, :], q)
            s = jnp.where(sub + t * tile <= limit, s, -jnp.inf)
            s_ref[span, :] = s
            top = jnp.maximum(top, jnp.max(s, axis=0, keepdims=True))
        total = jnp.zeros((1, rows), jnp.float32)
        for t in range(tiles):
            span = pl.ds(t * tile, tile)
            e = jnp.exp2((s_ref[span, :] - top) * (scale * math.log2(math.e)))
            s_ref[span, :] = e
            total = total + jnp.sum(e, axis=0, keepdims=True)
        inv = 1.0 / total
        delta = jnp.zeros((1, rows), jnp.float32)
        for t in range(tiles):
            span = pl.ds(t * tile, tile)
            p = s_ref[span, :] * inv
            pb = p.astype(jnp.bfloat16)
            dp = nt_dot(v_ref[span, :], g)
            s_ref[span, :] = p
            pb_ref[span, :] = pb
            dp_ref[span, :] = dp
            delta = delta + jnp.sum(pb.astype(jnp.float32) * dp, axis=0, keepdims=True)
        gq_t = jnp.zeros((hd, rows), jnp.float32)
        for t in range(tiles):
            span = pl.ds(t * tile, tile)
            ds = (s_ref[span, :] * (dp_ref[span, :] - delta)).astype(jnp.bfloat16)
            gq_t = gq_t + jnp.dot(kt_ref[:, span], ds, preferred_element_type=jnp.float32)
            gk_acc[span, :] += jnp.dot(ds, q, preferred_element_type=jnp.float32)
            gv_acc[span, :] += jnp.dot(pb_ref[span, :], g, preferred_element_type=jnp.float32)
        gq = jnp.transpose(gq_t * scale).astype(jnp.bfloat16)
        send_q[step] = gq.reshape(GROUP, toks, hd)
        exchange(
            step, source, lambda dev, other: send_q.at[step, other], recv_q.at[me],
            send_sem.at[1], recv_q_sem, step == 3,
        )

    for step, (dy, dh) in enumerate(STEPS):
        target = group_of(dy, dh)
        span = pl.ds(pl.multiple_of(target * rows, rows), rows)
        owners = pl.ds(target * GROUP, GROUP)
        send_kv[owners, 0:toks, :] = (
            (gk_acc[span, :] * scale).astype(jnp.bfloat16).reshape(GROUP, toks, hd)
        )
        send_kv[owners, toks : 2 * toks, :] = (
            gv_acc[span, :].astype(jnp.bfloat16).reshape(GROUP, toks, hd)
        )
        exchange(
            step, target, lambda dev, other: send_kv.at[dev], recv_kv.at[me],
            send_sem.at[2], recv_kv_sem.at[step], step == 3,
        )

    pltpu.make_async_copy(recv_q, recv_q, recv_q_sem).wait()
    for i in range(devices // GROUP):
        heads = pl.ds(i * GROUP, GROUP)
        gq_out[:, heads, :] = swap(recv_q[heads, :, :])
    for step, (dy, dh) in enumerate(STEPS):
        source = group_of(dy, dh)
        heads = pl.ds(pl.multiple_of(source * GROUP, GROUP), GROUP)
        pltpu.make_async_copy(
            recv_kv.at[heads], recv_kv.at[heads], recv_kv_sem.at[step]
        ).wait()
        gk_out[:, heads, :] = swap(recv_kv[heads, 0:toks, :])
        gv_out[:, heads, :] = swap(recv_kv[heads, toks : 2 * toks, :])
    for i, buf in enumerate((send_a, recv_q, send_kv)):
        sent = buf.at[pl.ds(0, devices - 1)]
        pltpu.make_async_copy(sent, sent, send_sem.at[i]).wait()


def body(queries, grad_out, keys, values, block_offsets):
    blocks, tok, heads, hd = queries.shape
    key_len = keys.shape[0]
    toks = blocks * tok
    rows = GROUP * toks
    bf16, f32 = jnp.bfloat16, jnp.float32
    vmem = pl.BlockSpec(memory_space=pltpu.VMEM)
    hbm = pl.BlockSpec(memory_space=pl.ANY)
    out = jax.ShapeDtypeStruct((toks, heads, hd), bf16)
    gq, gk, gv = pl.pallas_call(
        kernel,
        out_shape=(out, out, out),
        in_specs=[pl.BlockSpec(memory_space=pltpu.SMEM), hbm, hbm, hbm, hbm],
        out_specs=(vmem, vmem, vmem),
        scratch_shapes=[
            pltpu.VMEM((toks, heads, hd), bf16),
            pltpu.VMEM((toks, heads, hd), bf16),
            pltpu.VMEM((key_len, hd), bf16),
            pltpu.VMEM((key_len, hd), bf16),
            pltpu.VMEM((hd, key_len), bf16),
            pltpu.VMEM((heads, 2 * toks, hd), bf16),
            pltpu.VMEM((heads // GROUP, GROUP, 2 * toks, hd), bf16),
            pltpu.VMEM((heads // GROUP, GROUP, toks, hd), bf16),
            pltpu.VMEM((heads, toks, hd), bf16),
            pltpu.VMEM((heads, 2 * toks, hd), bf16),
            pltpu.VMEM((heads, 2 * toks, hd), bf16),
            pltpu.VMEM((key_len, rows), f32),
            pltpu.VMEM((key_len, rows), f32),
            pltpu.VMEM((key_len, rows), bf16),
            pltpu.VMEM((key_len, hd), f32),
            pltpu.VMEM((key_len, hd), f32),
            pltpu.SemaphoreType.DMA((4,)),
            pltpu.SemaphoreType.DMA((3,)),
            pltpu.SemaphoreType.DMA((4,)),
            pltpu.SemaphoreType.DMA,
            pltpu.SemaphoreType.DMA((4,)),
        ],
        compiler_params=pltpu.CompilerParams(
            collective_id=0, has_side_effects=True, vmem_limit_bytes=32 << 20
        ),
        cost_estimate=pl.CostEstimate(
            flops=12 * blocks * tok * heads * key_len * hd,
            bytes_accessed=14 * toks * heads * hd,
            transcendentals=blocks * tok * heads * key_len,
        ),
        name="backward",
    )(
        block_offsets,
        queries.reshape(toks, heads, hd),
        grad_out.reshape(toks, heads, hd),
        keys.reshape(key_len, hd),
        values.reshape(key_len, hd),
    )
    return gq.reshape(blocks, tok, heads, hd), gk, gv


def solution(mesh):
    in_specs = (
        P("batch", "seq", None, None),
        P("batch", "seq", None, None),
        P("batch", "seq", None),
        P("batch", "seq", None),
        P("batch"),
    )
    out_specs = (
        P("batch", "seq", None, None),
        P(("batch", "seq"), None, None),
        P(("batch", "seq"), None, None),
    )
    return jax.shard_map(body, mesh=mesh, in_specs=in_specs, out_specs=out_specs, check_vma=False)
```

time: 248 us -> 93.9 us (0.38)
  waiting for transfers between devices: 132 us -> 0 us
  Pallas kernels: 0 us -> 86.4 us
  starting transfers between devices: 65 us -> 0 us
  matrix products: 15.4 us -> 0 us
  local copies, waits for them, and re-layouts: 20.5 us -> 6.56 us
  other arithmetic: 12.8 us -> 0 us
    all_to_all x8 -> x0, waiting for transfers between devices: 132 us -> none  [the longest x2 36.8 us: body(): lax.all_to_all(grad_out[block], 'seq', split_axis=1, concat_axis=0, tiled...]
    pallas_call x0 -> x1, Pallas kernels: none -> 86.4 us  [body(): pl.pallas_call(kernel, out_shape=(out, out, out), in_specs=[pl.BlockSpec(...]
    all_to_all x8 -> x0, starting transfers between devices: 65 us -> none  [the longest x2 31.3 us: body(): lax.all_to_all(queries[block], 'seq', split_axis=1, concat_axis=0, tiled=...]
    dot_general x12 -> x0, matrix products: 15.4 us -> none  [the longest x2 3.8 us: block_backward(): jnp.einsum('hqk,qhd->khd', grad_scores, q_head, preferred_element_type=jn...]
    unnamed x34 -> x13, local copies, waits for them, and re-layouts: 14.9 us -> 6.56 us
    convert_element_type x5 -> x0, other arithmetic: 6.43 us -> none  [the longest x1 2.24 us: block_backward(): grad_q = (jnp.einsum('hqk,khd->qhd', grad_scores, keys, preferred_element...]
    unnamed x1 -> x0, other arithmetic: 2.95 us -> none
    slice x4 -> x0, local copies, waits for them, and re-layouts: 2.76 us -> none  [the longest x1 1.03 us: body(): queries[block]]
  transfers between devices with their start and end apart: 8 -> 0, of which waited for: 8 -> 0; matrix products, arithmetic and copies ran while one was open for 18% -> 0% of each run, Pallas kernels for 0% -> 0%
where the time goes in v1:
time: 93.9 us; the launch traced here: 93.6 us
  Pallas kernels  86.4 us (92%)
  local copies, waits for them, and re-layouts  6.56 us (7%)
    pallas_call x1, Pallas kernels, body(): pl.pallas_call(kernel, out_shape=(out, out, out), in_specs=[pl.BlockSpec(...  86.4 us
    unnamed x13, local copies, waits for them, and re-layouts  6.56 us

profile of v1, /device:TPU:1, one launch (start us, length us, event | category | flops | bytes accessed | tf_op | source)
XLA Modules:
  0.0 93.6 jit_solution(12890416642523974457)
XLA Ops:
  0.6 0.0 copy-start.4
  0.6 0.6 copy-done.4
  1.3 0.0 copy-start
  1.3 0.9 %copy-done = bf16[2,8,64,128]{3,2,1,0:T(8,128)(2,1)S(1)} copy-done((bf16[2,8,64,128]{3,2,1,0:T(8,128)(2,1)S(1)}, bf16[2,8,64,128]{3,2,1,0:T(8,128)(2,1)}, u32[]{:S(2)}) %copy-start) | copy-done | bytes 262168
  2.2 0.0 copy-start.1
  2.2 0.9 %copy-done.1 = bf16[2,8,64,128]{3,2,1,0:T(8,128)(2,1)S(1)} copy-done((bf16[2,8,64,128]{3,2,1,0:T(8,128)(2,1)S(1)}, bf16[2,8,64,128]{3,2,1,0:T(8,128)(2,1)}, u32[]{:S(2)}) %copy-start.1) | copy-done | bytes 262168
  3.2 0.0 copy-start.2
  3.2 0.9 %copy-done.2 = bf16[1024,1,128]{2,0,1:T(8,128)(2,1)S(1)} copy-done((bf16[1024,1,128]{2,0,1:T(8,128)(2,1)S(1)}, bf16[1024,1,128]{2,0,1:T(8,128)(2,1)}, u32[]{:S(2)}) %copy-start.2) | copy-done | bytes 262168
  4.1 0.0 copy-start.3
  4.1 0.9 %copy-done.3 = bf16[1024,1,128]{2,0,1:T(8,128)(2,1)S(1)} copy-done((bf16[1024,1,128]{2,0,1:T(8,128)(2,1)S(1)}, bf16[1024,1,128]{2,0,1:T(8,128)(2,1)}, u32[]{:S(2)}) %copy-start.3) | copy-done | bytes 262168
  5.1 86.4 %backward.1 = (bf16[16,64,128]{2,1,0:T(8,128)(2,1)S(1)}, bf16[16,64,128]{2,1,0:T(8,128)(2,1)S(1)}, bf16[16,64,128]{2,1,0:T(8,128)(2,1)S(1)}) custom-call(s32[3]{0:T(128)S(1)} %copy-done.4, bf16[16,64,128]{2,1,0:T(8,128)(2,1)S(1)} %bitcast.6, bf16[16,64,128]{2,1,0:T(8,128)(2,1)S(1)} %bitcast.7, bf16[1024,128]{1,0:T(8,128)(2,1)S(1)} %bitcast.8, ...), custom_call_target="tpu_custom_call" | custom-call | flops 1610612736 | bytes 1835008 | tf_op jit(solution)/shard_map/backward/pallas_call | solution.py:193
  91.5 0.7 copy.11
  92.2 0.7 copy.12
  92.9 0.7 copy.13
Async XLA Ops:
  0.6 0.7 copy-start.4
  1.3 0.9 %copy-start = (bf16[2,8,64,128]{3,2,1,0:T(8,128)(2,1)S(1)}, bf16[2,8,64,128]{3,2,1,0:T(8,128)(2,1)}, u32[]{:S(2)}) copy-start(bf16[2,8,64,128]{3,2,1,0:T(8,128)(2,1)} %param.5) | copy-start | bytes 786436
  2.2 0.9 %copy-start.1 = (bf16[2,8,64,128]{3,2,1,0:T(8,128)(2,1)S(1)}, bf16[2,8,64,128]{3,2,1,0:T(8,128)(2,1)}, u32[]{:S(2)}) copy-start(bf16[2,8,64,128]{3,2,1,0:T(8,128)(2,1)} %param.6) | copy-start | bytes 786436
  3.2 0.9 %copy-start.2 = (bf16[1024,1,128]{2,0,1:T(8,128)(2,1)S(1)}, bf16[1024,1,128]{2,0,1:T(8,128)(2,1)}, u32[]{:S(2)}) copy-start(bf16[1024,1,128]{2,0,1:T(8,128)(2,1)} %param.7) | copy-start | bytes 786436
  4.1 0.9 %copy-start.3 = (bf16[1024,1,128]{2,0,1:T(8,128)(2,1)S(1)}, bf16[1024,1,128]{2,0,1:T(8,128)(2,1)}, u32[]{:S(2)}) copy-start(bf16[1024,1,128]{2,0,1:T(8,128)(2,1)} %param.8) | copy-start | bytes 786436

commit v2 on v1

--- a/solution.py
+++ b/solution.py
@@ -11,6 +11,8 @@
 MESH = pl.DeviceIdType.MESH
 GROUP = 16
 STEPS = ((1, 1), (0, 1), (1, 0), (0, 0))
+ASTEPS = ((1, 0), (1, 1), (0, 1), (0, 0))
+MIB = 1 << 20
 
 
 def nt_dot(a, b):
@@ -22,11 +24,11 @@
 
 
 def kernel(
-    offs, q_hbm, g_hbm, k_hbm, v_hbm, gq_out, gk_out, gv_out,
-    q_in, g_in, k_ref, v_ref, kt_ref,
-    send_a, recv_a, send_q, recv_q, send_kv, recv_kv,
+    offs_hbm, q_hbm, g_hbm, k_hbm, v_hbm, out_hbm,
+    offs, q_in, g_in, k_ref, v_ref, kt_ref,
+    send_a, recv_a, send_q, recv_q, send_kv, recv_kv, gq_out, gk_out, gv_out,
     s_ref, dp_ref, pb_ref, gk_acc, gv_acc,
-    in_sem, send_sem, recv_a_sem, recv_q_sem, recv_kv_sem,
+    in_sem, send_sem, recv_a_sem, recv_q_sem, recv_kv_sem, out_sem,
 ):
     devices = send_a.shape[0]
     toks = q_in.shape[0]
@@ -44,24 +46,27 @@
     def group_of(dy, dh):
         return lax.rem(gy + dy, 2) * 2 + lax.rem(gh + dh, 2)
 
+    barrier = pltpu.get_barrier_semaphore()
+    for step, (dy, dh) in enumerate(STEPS):
+        target = group_of(dy, dh)
+
+        def greet(i, carry):
+            pl.semaphore_signal(
+                barrier, inc=1, device_id={"seq": target * GROUP + lax.rem(pos + i, GROUP)},
+                device_id_type=MESH,
+            )
+            return carry
+
+        lax.fori_loop(1 if step == 3 else 0, GROUP, greet, 0)
+
     loads = [
         pltpu.make_async_copy(src, dst, in_sem.at[i])
         for i, (src, dst) in enumerate(
-            ((q_hbm, q_in), (g_hbm, g_in), (k_hbm, k_ref), (v_hbm, v_ref))
+            ((q_hbm, q_in), (g_hbm, g_in), (k_hbm, k_ref), (v_hbm, v_ref), (offs_hbm, offs))
         )
     ]
     for load in loads:
         load.start()
-
-    barrier = pltpu.get_barrier_semaphore()
-
-    def greet(i, carry):
-        pl.semaphore_signal(
-            barrier, inc=1, device_id={"seq": lax.rem(me + i, devices)}, device_id_type=MESH
-        )
-        return carry
-
-    lax.fori_loop(1, devices, greet, 0)
     loads[0].wait()
     loads[1].wait()
 
@@ -79,7 +84,7 @@
             pltpu.make_async_copy(src(me, pos), dst, r_sem).start()
         lax.fori_loop(1 if own else 0, GROUP, one, 0)
 
-    for step, (dy, dh) in enumerate(STEPS):
+    for step, (dy, dh) in enumerate(ASTEPS):
         target = group_of(dy, dh)
         heads = pl.ds(pl.multiple_of(target * GROUP, GROUP), GROUP)
         send_a[heads, 0:toks, :] = swap(q_in[:, heads, :])
@@ -91,8 +96,8 @@
             send_sem.at[0], recv_a_sem.at[step], step == 3,
         )
 
-    loads[2].wait()
-    loads[3].wait()
+    for load in loads[2:]:
+        load.wait()
     for t in range(tiles):
         span = pl.ds(t * tile, tile)
         kt_ref[:, span] = jnp.transpose(k_ref[span, :].astype(jnp.float32)).astype(jnp.bfloat16)
@@ -105,7 +110,7 @@
     shift = jnp.where(in_tok >= half, offs[2], offs[1]) - offs[0]
     local_pos = shift + (lane // toks) * half + in_tok % half
 
-    for step, (dy, dh) in enumerate(STEPS):
+    for step, (dy, dh) in enumerate(ASTEPS):
         source = group_of(dy, dh)
         pltpu.make_async_copy(recv_a.at[step], recv_a.at[step], recv_a_sem.at[step]).wait()
         q = recv_a[step, :, 0:toks, :].reshape(rows, hd)
@@ -164,10 +169,19 @@
             send_sem.at[2], recv_kv_sem.at[step], step == 3,
         )
 
+    stores = []
+
+    def store(i, staged, out, heads):
+        stores.append(
+            pltpu.make_async_copy(staged.at[:, heads, :], out.at[:, heads, :], out_sem.at[i])
+        )
+        stores[-1].start()
+
     pltpu.make_async_copy(recv_q, recv_q, recv_q_sem).wait()
     for i in range(devices // GROUP):
         heads = pl.ds(i * GROUP, GROUP)
         gq_out[:, heads, :] = swap(recv_q[heads, :, :])
+        store(i, gq_out, out_hbm.at[0], heads)
     for step, (dy, dh) in enumerate(STEPS):
         source = group_of(dy, dh)
         heads = pl.ds(pl.multiple_of(source * GROUP, GROUP), GROUP)
@@ -175,7 +189,11 @@
             recv_kv.at[heads], recv_kv.at[heads], recv_kv_sem.at[step]
         ).wait()
         gk_out[:, heads, :] = swap(recv_kv[heads, 0:toks, :])
+        store(4 + step, gk_out, out_hbm.at[1], heads)
         gv_out[:, heads, :] = swap(recv_kv[heads, toks : 2 * toks, :])
+        store(8 + step, gv_out, out_hbm.at[2], heads)
+    for copy in stores:
+        copy.wait()
     for i, buf in enumerate((send_a, recv_q, send_kv)):
         sent = buf.at[pl.ds(0, devices - 1)]
         pltpu.make_async_copy(sent, sent, send_sem.at[i]).wait()
@@ -187,15 +205,14 @@
     toks = blocks * tok
     rows = GROUP * toks
     bf16, f32 = jnp.bfloat16, jnp.float32
-    vmem = pl.BlockSpec(memory_space=pltpu.VMEM)
     hbm = pl.BlockSpec(memory_space=pl.ANY)
-    out = jax.ShapeDtypeStruct((toks, heads, hd), bf16)
-    gq, gk, gv = pl.pallas_call(
+    grads = pl.pallas_call(
         kernel,
-        out_shape=(out, out, out),
-        in_specs=[pl.BlockSpec(memory_space=pltpu.SMEM), hbm, hbm, hbm, hbm],
-        out_specs=(vmem, vmem, vmem),
+        out_shape=jax.ShapeDtypeStruct((3, toks, heads, hd), bf16),
+        in_specs=[hbm] * 5,
+        out_specs=hbm,
         scratch_shapes=[
+            pltpu.SMEM((1 + blocks,), jnp.int32),
             pltpu.VMEM((toks, heads, hd), bf16),
             pltpu.VMEM((toks, heads, hd), bf16),
             pltpu.VMEM((key_len, hd), bf16),
@@ -207,19 +224,23 @@
             pltpu.VMEM((heads, toks, hd), bf16),
             pltpu.VMEM((heads, 2 * toks, hd), bf16),
             pltpu.VMEM((heads, 2 * toks, hd), bf16),
+            pltpu.VMEM((toks, heads, hd), bf16),
+            pltpu.VMEM((toks, heads, hd), bf16),
+            pltpu.VMEM((toks, heads, hd), bf16),
             pltpu.VMEM((key_len, rows), f32),
             pltpu.VMEM((key_len, rows), f32),
             pltpu.VMEM((key_len, rows), bf16),
             pltpu.VMEM((key_len, hd), f32),
             pltpu.VMEM((key_len, hd), f32),
-            pltpu.SemaphoreType.DMA((4,)),
+            pltpu.SemaphoreType.DMA((5,)),
             pltpu.SemaphoreType.DMA((3,)),
             pltpu.SemaphoreType.DMA((4,)),
             pltpu.SemaphoreType.DMA,
             pltpu.SemaphoreType.DMA((4,)),
+            pltpu.SemaphoreType.DMA((12,)),
         ],
         compiler_params=pltpu.CompilerParams(
-            collective_id=0, has_side_effects=True, vmem_limit_bytes=32 << 20
+            collective_id=0, has_side_effects=True, vmem_limit_bytes=60 * MIB
         ),
         cost_estimate=pl.CostEstimate(
             flops=12 * blocks * tok * heads * key_len * hd,
@@ -234,7 +255,7 @@
         keys.reshape(key_len, hd),
         values.reshape(key_len, hd),
     )
-    return gq.reshape(blocks, tok, heads, hd), gk, gv
+    return grads[0].reshape(blocks, tok, heads, hd), grads[1], grads[2]
 
 
 def solution(mesh):

time: 93.9 us -> 89.2 us (0.950)
  the two profiles are of different devices: /device:TPU:1 before, /device:TPU:64 now
where the time goes in v2:
time: 89.2 us; the launch traced here: 89.1 us
  Pallas kernels  86.4 us (97%)
  local copies, waits for them, and re-layouts  2 us (2%)
    pallas_call x1, Pallas kernels, body(): pl.pallas_call(kernel, out_shape=jax.ShapeDtypeStruct((3, toks, heads, hd...  86.4 us
    squeeze x1, local copies, waits for them, and re-layouts, body(): return (grads[0].reshape(blocks, tok, heads, hd), grads[1], grads[2])  2 us

profile of v2, /device:TPU:64, one launch (start us, length us, event | category | flops | bytes accessed | tf_op | source)
XLA Modules:
  0.0 89.1 jit_solution(11456501255306072296)
XLA Ops:
  0.6 86.4 %backward.1 = bf16[3,16,64,128]{3,2,1,0:T(8,128)(2,1)} custom-call(s32[3]{0:T(128)} %offs_hbm.1, bf16[16,64,128]{2,1,0:T(8,128)(2,1)} %bitcast.10, bf16[16,64,128]{2,1,0:T(8,128)(2,1)} %bitcast.11, bf16[1024,128]{1,0:T(8,128)(2,1)} %bitcast.12, bf16[1024,128]{1,0:T(8,128)(2,1)} %bitcast.13), custom_call_target="tpu_custom_call" | custom-call | flops 1610612736 | bytes 1835008 | tf_op jit(solution)/shard_map/backward/pallas_call | solution.py:209
  87.1 2.0 %slice_bitcast_fusion = (bf16[16,64,128]{2,1,0:T(8,128)(2,1)}, bf16[16,64,128]{2,1,0:T(8,128)(2,1)}, bf16[1,16,64,128]{3,2,1,0:T(8,128)(2,1)}) fusion(bf16[3,16,64,128]{3,2,1,0:T(8,128)(2,1)} %backward.1), kind=kLoop, calls=%fused_computation | loop fusion | bytes 1572864 | tf_op jit(solution)/shard_map/squeeze | solution.py:258

commit v3 on v2

--- a/solution.py
+++ b/solution.py
@@ -10,8 +10,6 @@
 
 MESH = pl.DeviceIdType.MESH
 GROUP = 16
-STEPS = ((1, 1), (0, 1), (1, 0), (0, 0))
-ASTEPS = ((1, 0), (1, 1), (0, 1), (0, 0))
 MIB = 1 << 20
 
 
@@ -40,24 +38,28 @@
     scale = hd ** -0.5
 
     me = lax.axis_index("seq")
-    group, pos = me // GROUP, me % GROUP
-    gy, gh = group // 2, group % 2
-
-    def group_of(dy, dh):
-        return lax.rem(gy + dy, 2) * 2 + lax.rem(gh + dh, 2)
+    slots = devices // GROUP
+    ring = devices // 4
+    my_y, my_z, my_c = me // (2 * ring), (me // 2) % ring, me % 2
+
+    def partner(slot, i, sign):
+        p = (slot % 2) * (GROUP // 2) + i // 2
+        dz = (1 - p % 2) * (ring // 2 + p // 2) + (p % 2) * (ring // 2 - (p + 1) // 2)
+        y = 1 - my_y if slot < 2 else my_y
+        z = (my_z + ring + sign * dz) % ring
+        c = (my_c + 1 + i % 2) % 2
+        return (y * ring + z) * 2 + c
 
     barrier = pltpu.get_barrier_semaphore()
-    for step, (dy, dh) in enumerate(STEPS):
-        target = group_of(dy, dh)
+    for slot in range(slots):
 
         def greet(i, carry):
             pl.semaphore_signal(
-                barrier, inc=1, device_id={"seq": target * GROUP + lax.rem(pos + i, GROUP)},
-                device_id_type=MESH,
+                barrier, inc=1, device_id={"seq": partner(slot, i, 1)}, device_id_type=MESH
             )
             return carry
 
-        lax.fori_loop(1 if step == 3 else 0, GROUP, greet, 0)
+        lax.fori_loop(0, GROUP - (slot == slots - 1), greet, 0)
 
     loads = [
         pltpu.make_async_copy(src, dst, in_sem.at[i])
@@ -70,30 +72,29 @@
     loads[0].wait()
     loads[1].wait()
 
-    def exchange(step, target, src, dst, s_sem, r_sem, own):
+    def exchange(slot, sign, src, dst, s_sem, r_sem):
         def one(i, carry):
-            other = lax.rem(pos + i, GROUP)
-            dev = target * GROUP + other
+            dev = partner(slot, i, sign)
             pltpu.make_async_remote_copy(
-                src_ref=src(dev, other), dst_ref=dst, send_sem=s_sem, recv_sem=r_sem,
+                src_ref=src(dev, i), dst_ref=dst(i), send_sem=s_sem, recv_sem=r_sem,
                 device_id={"seq": dev}, device_id_type=MESH,
             ).start()
             return carry
 
+        own = slot == slots - 1
+        lax.fori_loop(0, GROUP - own, one, 0)
         if own:
-            pltpu.make_async_copy(src(me, pos), dst, r_sem).start()
-        lax.fori_loop(1 if own else 0, GROUP, one, 0)
-
-    for step, (dy, dh) in enumerate(ASTEPS):
-        target = group_of(dy, dh)
-        heads = pl.ds(pl.multiple_of(target * GROUP, GROUP), GROUP)
+            pltpu.make_async_copy(src(me, GROUP - 1), dst(GROUP - 1), r_sem).start()
+
+    for i in range(slots):
+        heads = pl.ds(i * GROUP, GROUP)
         send_a[heads, 0:toks, :] = swap(q_in[:, heads, :])
         send_a[heads, toks : 2 * toks, :] = swap(g_in[:, heads, :])
-        if step == 0:
-            pl.semaphore_wait(barrier, devices - 1)
+    pl.semaphore_wait(barrier, devices - 1)
+    for slot in range(slots):
         exchange(
-            step, target, lambda dev, other: send_a.at[dev], recv_a.at[step, pos],
-            send_sem.at[0], recv_a_sem.at[step], step == 3,
+            slot, 1, lambda dev, i: send_a.at[dev], lambda i: recv_a.at[slot, i],
+            send_sem.at[0], recv_a_sem.at[slot],
         )
 
     for load in loads[2:]:
@@ -108,14 +109,13 @@
     sub = lax.broadcasted_iota(jnp.int32, (tile, rows), 0)
     in_tok = lane % toks
     shift = jnp.where(in_tok >= half, offs[2], offs[1]) - offs[0]
-    local_pos = shift + (lane // toks) * half + in_tok % half
-
-    for step, (dy, dh) in enumerate(ASTEPS):
-        source = group_of(dy, dh)
+    local_pos = shift + in_tok % half
+
+    for step in range(slots):
         pltpu.make_async_copy(recv_a.at[step], recv_a.at[step], recv_a_sem.at[step]).wait()
         q = recv_a[step, :, 0:toks, :].reshape(rows, hd)
         g = recv_a[step, :, toks : 2 * toks, :].reshape(rows, hd)
-        limit = local_pos + source * (GROUP * half)
+        limit = local_pos + half * partner(step, lane // toks, -1)
         top = jnp.full((1, rows), -jnp.inf, jnp.float32)
         for t in range(tiles):
             span = pl.ds(t * tile, tile)
@@ -150,23 +150,24 @@
         gq = jnp.transpose(gq_t * scale).astype(jnp.bfloat16)
         send_q[step] = gq.reshape(GROUP, toks, hd)
         exchange(
-            step, source, lambda dev, other: send_q.at[step, other], recv_q.at[me],
-            send_sem.at[1], recv_q_sem, step == 3,
-        )
-
-    for step, (dy, dh) in enumerate(STEPS):
-        target = group_of(dy, dh)
-        span = pl.ds(pl.multiple_of(target * rows, rows), rows)
-        owners = pl.ds(target * GROUP, GROUP)
+            step, -1, lambda dev, i: send_q.at[step, i], lambda i: recv_q.at[me],
+            send_sem.at[1], recv_q_sem,
+        )
+
+    for i in range(slots):
+        span = pl.ds(i * rows, rows)
+        owners = pl.ds(i * GROUP, GROUP)
         send_kv[owners, 0:toks, :] = (
             (gk_acc[span, :] * scale).astype(jnp.bfloat16).reshape(GROUP, toks, hd)
         )
         send_kv[owners, toks : 2 * toks, :] = (
             gv_acc[span, :].astype(jnp.bfloat16).reshape(GROUP, toks, hd)
         )
+    group = me // GROUP
+    for slot in range(slots):
         exchange(
-            step, target, lambda dev, other: send_kv.at[dev], recv_kv.at[me],
-            send_sem.at[2], recv_kv_sem.at[step], step == 3,
+            slot, 1, lambda dev, i: send_kv.at[dev], lambda i: recv_kv.at[me],
+            send_sem.at[2], recv_kv_sem.at[group],
         )
 
     stores = []
@@ -182,11 +183,11 @@
         heads = pl.ds(i * GROUP, GROUP)
         gq_out[:, heads, :] = swap(recv_q[heads, :, :])
         store(i, gq_out, out_hbm.at[0], heads)
-    for step, (dy, dh) in enumerate(STEPS):
-        source = group_of(dy, dh)
+    for step, ahead in enumerate((2, 3, 1, 0)):
+        source = (group // 2 + ahead // 2) % 2 * 2 + (group + ahead) % 2
         heads = pl.ds(pl.multiple_of(source * GROUP, GROUP), GROUP)
         pltpu.make_async_copy(
-            recv_kv.at[heads], recv_kv.at[heads], recv_kv_sem.at[step]
+            recv_kv.at[heads], recv_kv.at[heads], recv_kv_sem.at[source]
         ).wait()
         gk_out[:, heads, :] = swap(recv_kv[heads, 0:toks, :])
         store(4 + step, gk_out, out_hbm.at[1], heads)

time: 89.2 us -> 87.5 us (0.981)
  the two profiles are of different devices: /device:TPU:64 before, /device:TPU:1 now
where the time goes in v3:
time: 87.5 us; the launch traced here: 87.3 us
  Pallas kernels  84.7 us (97%)
  local copies, waits for them, and re-layouts  2 us (2%)
    pallas_call x1, Pallas kernels, body(): pl.pallas_call(kernel, out_shape=jax.ShapeDtypeStruct((3, toks, heads, hd...  84.7 us
    squeeze x1, local copies, waits for them, and re-layouts, body(): return (grads[0].reshape(blocks, tok, heads, hd), grads[1], grads[2])  2 us

profile of v3, /device:TPU:1, one launch (start us, length us, event | category | flops | bytes accessed | tf_op | source)
XLA Modules:
  0.0 87.3 jit_solution(14412572717194312562)
XLA Ops:
  0.6 84.7 %backward.1 = bf16[3,16,64,128]{3,2,1,0:T(8,128)(2,1)} custom-call(s32[3]{0:T(128)} %offs_hbm.1, bf16[16,64,128]{2,1,0:T(8,128)(2,1)} %bitcast.10, bf16[16,64,128]{2,1,0:T(8,128)(2,1)} %bitcast.11, bf16[1024,128]{1,0:T(8,128)(2,1)} %bitcast.12, bf16[1024,128]{1,0:T(8,128)(2,1)} %bitcast.13), custom_call_target="tpu_custom_call" | custom-call | flops 1610612736 | bytes 1835008 | tf_op jit(solution)/shard_map/backward/pallas_call | solution.py:210
  85.3 2.0 %slice_bitcast_fusion = (bf16[16,64,128]{2,1,0:T(8,128)(2,1)}, bf16[16,64,128]{2,1,0:T(8,128)(2,1)}, bf16[1,16,64,128]{3,2,1,0:T(8,128)(2,1)}) fusion(bf16[3,16,64,128]{3,2,1,0:T(8,128)(2,1)} %backward.1), kind=kLoop, calls=%fused_computation | loop fusion | bytes 1572864 | tf_op jit(solution)/shard_map/squeeze | solution.py:259

commit v4 on v3

--- a/solution.py
+++ b/solution.py
@@ -22,9 +22,9 @@
 
 
 def kernel(
-    offs_hbm, q_hbm, g_hbm, k_hbm, v_hbm, out_hbm,
+    offs_hbm, q_hbm, g_hbm, k_hbm, v_hbm, gq_hbm, recv_kv,
     offs, q_in, g_in, k_ref, v_ref, kt_ref,
-    send_a, recv_a, send_q, recv_q, send_kv, recv_kv, gq_out, gk_out, gv_out,
+    send_a, recv_a, send_q, recv_q, send_kv, gq_out,
     s_ref, dp_ref, pb_ref, gk_acc, gv_acc,
     in_sem, send_sem, recv_a_sem, recv_q_sem, recv_kv_sem, out_sem,
 ):
@@ -42,24 +42,33 @@
     ring = devices // 4
     my_y, my_z, my_c = me // (2 * ring), (me // 2) % ring, me % 2
 
-    def partner(slot, i, sign):
-        p = (slot % 2) * (GROUP // 2) + i // 2
-        dz = (1 - p % 2) * (ring // 2 + p // 2) + (p % 2) * (ring // 2 - (p + 1) // 2)
+    def partner(slot, j, m, sign):
+        k = (slot % 2) * (GROUP // 4) + j
+        dz = ring // 2 + k if m < 2 else ring // 2 - 1 - k
         y = 1 - my_y if slot < 2 else my_y
-        z = (my_z + ring + sign * dz) % ring
-        c = (my_c + 1 + i % 2) % 2
+        z = lax.rem(my_z + dz if sign > 0 else my_z + ring - dz, ring)
+        c = 1 - my_c if m % 2 == 0 else my_c
         return (y * ring + z) * 2 + c
+
+    def each(slot, sign, act):
+        def four(j, carry):
+            for m in range(4):
+                act(partner(slot, j, m, sign), 4 * j + m)
+            return carry
+
+        last = GROUP // 4 - 1
+        if slot < slots - 1:
+            lax.fori_loop(0, last + 1, four, 0)
+        else:
+            lax.fori_loop(0, last, four, 0)
+            for m in range(3):
+                act(partner(slot, last, m, sign), 4 * last + m)
 
     barrier = pltpu.get_barrier_semaphore()
     for slot in range(slots):
-
-        def greet(i, carry):
-            pl.semaphore_signal(
-                barrier, inc=1, device_id={"seq": partner(slot, i, 1)}, device_id_type=MESH
-            )
-            return carry
-
-        lax.fori_loop(0, GROUP - (slot == slots - 1), greet, 0)
+        each(slot, 1, lambda dev, i: pl.semaphore_signal(
+            barrier, inc=1, device_id={"seq": dev}, device_id_type=MESH
+        ))
 
     loads = [
         pltpu.make_async_copy(src, dst, in_sem.at[i])
@@ -73,17 +82,14 @@
     loads[1].wait()
 
     def exchange(slot, sign, src, dst, s_sem, r_sem):
-        def one(i, carry):
-            dev = partner(slot, i, sign)
+        def one(dev, i):
             pltpu.make_async_remote_copy(
                 src_ref=src(dev, i), dst_ref=dst(i), send_sem=s_sem, recv_sem=r_sem,
                 device_id={"seq": dev}, device_id_type=MESH,
             ).start()
-            return carry
-
-        own = slot == slots - 1
-        lax.fori_loop(0, GROUP - own, one, 0)
-        if own:
+
+        each(slot, sign, one)
+        if slot == slots - 1:
             pltpu.make_async_copy(src(me, GROUP - 1), dst(GROUP - 1), r_sem).start()
 
     for i in range(slots):
@@ -108,6 +114,7 @@
     lane = lax.broadcasted_iota(jnp.int32, (1, rows), 1)
     sub = lax.broadcasted_iota(jnp.int32, (tile, rows), 0)
     in_tok = lane % toks
+    number = lane // toks
     shift = jnp.where(in_tok >= half, offs[2], offs[1]) - offs[0]
     local_pos = shift + in_tok % half
 
@@ -115,7 +122,10 @@
         pltpu.make_async_copy(recv_a.at[step], recv_a.at[step], recv_a_sem.at[step]).wait()
         q = recv_a[step, :, 0:toks, :].reshape(rows, hd)
         g = recv_a[step, :, toks : 2 * toks, :].reshape(rows, hd)
-        limit = local_pos + half * partner(step, lane // toks, -1)
+        device = jnp.zeros_like(lane)
+        for m in range(4):
+            device = jnp.where(number % 4 == m, partner(step, number // 4, m, -1), device)
+        limit = local_pos + half * device
         top = jnp.full((1, rows), -jnp.inf, jnp.float32)
         for t in range(tiles):
             span = pl.ds(t * tile, tile)
@@ -163,11 +173,10 @@
         send_kv[owners, toks : 2 * toks, :] = (
             gv_acc[span, :].astype(jnp.bfloat16).reshape(GROUP, toks, hd)
         )
-    group = me // GROUP
     for slot in range(slots):
         exchange(
             slot, 1, lambda dev, i: send_kv.at[dev], lambda i: recv_kv.at[me],
-            send_sem.at[2], recv_kv_sem.at[group],
+            send_sem.at[2], recv_kv_sem,
         )
 
     stores = []
@@ -182,22 +191,43 @@
     for i in range(devices // GROUP):
         heads = pl.ds(i * GROUP, GROUP)
         gq_out[:, heads, :] = swap(recv_q[heads, :, :])
-        store(i, gq_out, out_hbm.at[0], heads)
-    for step, ahead in enumerate((2, 3, 1, 0)):
-        source = (group // 2 + ahead // 2) % 2 * 2 + (group + ahead) % 2
-        heads = pl.ds(pl.multiple_of(source * GROUP, GROUP), GROUP)
-        pltpu.make_async_copy(
-            recv_kv.at[heads], recv_kv.at[heads], recv_kv_sem.at[source]
-        ).wait()
-        gk_out[:, heads, :] = swap(recv_kv[heads, 0:toks, :])
-        store(4 + step, gk_out, out_hbm.at[1], heads)
-        gv_out[:, heads, :] = swap(recv_kv[heads, toks : 2 * toks, :])
-        store(8 + step, gv_out, out_hbm.at[2], heads)
+        store(i, gq_out, gq_hbm, heads)
+    pltpu.make_async_copy(recv_kv, recv_kv, recv_kv_sem).wait()
     for copy in stores:
         copy.wait()
     for i, buf in enumerate((send_a, recv_q, send_kv)):
         sent = buf.at[pl.ds(0, devices - 1)]
         pltpu.make_async_copy(sent, sent, send_sem.at[i]).wait()
+
+
+def by_token(gq_in, kv_in, gq_hbm, gk_hbm, gv_hbm, gq, kv, gk, gv, in_sem, out_sem):
+    toks = gq.shape[0]
+    slots = kv.shape[0] // GROUP
+    groups = [pl.ds(i * GROUP, GROUP) for i in range(slots)]
+    loads = [
+        pltpu.make_async_copy(kv_in.at[heads], kv.at[heads], in_sem.at[i])
+        for i, heads in enumerate(groups)
+    ]
+    loads.append(pltpu.make_async_copy(gq_in, gq, in_sem.at[slots]))
+    for load in loads:
+        load.start()
+    stores = []
+
+    def store(src, dst):
+        stores.append(pltpu.make_async_copy(src, dst, out_sem.at[len(stores)]))
+        stores[-1].start()
+
+    for i, heads in enumerate(groups):
+        loads[i].wait()
+        gk[:, heads, :] = swap(kv[heads, 0:toks, :])
+        store(gk.at[:, heads, :], gk_hbm.at[:, heads, :])
+        gv[:, heads, :] = swap(kv[heads, toks : 2 * toks, :])
+        store(gv.at[:, heads, :], gv_hbm.at[:, heads, :])
+        if i == 0:
+            loads[slots].wait()
+            store(gq, gq_hbm)
+    for copy in stores:
+        copy.wait()
 
 
 def body(queries, grad_out, keys, values, block_offsets):
@@ -207,11 +237,12 @@
     rows = GROUP * toks
     bf16, f32 = jnp.bfloat16, jnp.float32
     hbm = pl.BlockSpec(memory_space=pl.ANY)
-    grads = pl.pallas_call(
+    out = jax.ShapeDtypeStruct((toks, heads, hd), bf16)
+    gq, kv = pl.pallas_call(
         kernel,
-        out_shape=jax.ShapeDtypeStruct((3, toks, heads, hd), bf16),
+        out_shape=(out, jax.ShapeDtypeStruct((heads, 2 * toks, hd), bf16)),
         in_specs=[hbm] * 5,
-        out_specs=hbm,
+        out_specs=(hbm, hbm),
         scratch_shapes=[
             pltpu.SMEM((1 + blocks,), jnp.int32),
             pltpu.VMEM((toks, heads, hd), bf16),
@@ -224,9 +255,6 @@
             pltpu.VMEM((heads // GROUP, GROUP, toks, hd), bf16),
             pltpu.VMEM((heads, toks, hd), bf16),
             pltpu.VMEM((heads, 2 * toks, hd), bf16),
-            pltpu.VMEM((heads, 2 * toks, hd), bf16),
-            pltpu.VMEM((toks, heads, hd), bf16),
-            pltpu.VMEM((toks, heads, hd), bf16),
             pltpu.VMEM((toks, heads, hd), bf16),
             pltpu.VMEM((key_len, rows), f32),
             pltpu.VMEM((key_len, rows), f32),
@@ -237,8 +265,8 @@
             pltpu.SemaphoreType.DMA((3,)),
             pltpu.SemaphoreType.DMA((4,)),
             pltpu.SemaphoreType.DMA,
+            pltpu.SemaphoreType.DMA,
             pltpu.SemaphoreType.DMA((4,)),
-            pltpu.SemaphoreType.DMA((12,)),
         ],
         compiler_params=pltpu.CompilerParams(
             collective_id=0, has_side_effects=True, vmem_limit_bytes=60 * MIB
@@ -256,7 +284,22 @@
         keys.reshape(key_len, hd),
         values.reshape(key_len, hd),
     )
-    return grads[0].reshape(blocks, tok, heads, hd), grads[1], grads[2]
+    gq, gk, gv = pl.pallas_call(
+        by_token,
+        out_shape=(out, out, out),
+        in_specs=[hbm, hbm],
+        out_specs=(hbm, hbm, hbm),
+        scratch_shapes=[
+            pltpu.VMEM((toks, heads, hd), bf16),
+            pltpu.VMEM((heads, 2 * toks, hd), bf16),
+            pltpu.VMEM((toks, heads, hd), bf16),
+            pltpu.VMEM((toks, heads, hd), bf16),
+            pltpu.SemaphoreType.DMA((1 + heads // GROUP,)),
+            pltpu.SemaphoreType.DMA((1 + 2 * heads // GROUP,)),
+        ],
+        name="by_token",
+    )(gq, kv)
+    return gq.reshape(blocks, tok, heads, hd), gk, gv
 
 
 def solution(mesh):

time: 87.5 us -> 86.7 us (level)
  local copies, waits for them, and re-layouts: 2 us -> 0 us
  Pallas kernels: 84.7 us -> 85.9 us
    squeeze x1 -> x0, local copies, waits for them, and re-layouts: 2 us -> none  [body(): return (grads[0].reshape(blocks, tok, heads, hd), grads[1], grads[2])]
    pallas_call x1 -> x2, Pallas kernels: 84.7 us -> 85.9 us  [the longest x1 83.7 us: body(): pl.pallas_call(kernel, out_shape=(out, jax.ShapeDtypeStruct((heads, 2 * t...]
where the time goes in v4:
time: 86.7 us; the launch traced here: 86.5 us
  Pallas kernels  85.9 us (99%)
    pallas_call x1, Pallas kernels, body(): pl.pallas_call(kernel, out_shape=(out, jax.ShapeDtypeStruct((heads, 2 * t...  83.7 us
    pallas_call x1, Pallas kernels, body(): pl.pallas_call(by_token, out_shape=(out, out, out), in_specs=[hbm, hbm],...  2.15 us

profile of v4, /device:TPU:1, one launch (start us, length us, event | category | flops | bytes accessed | tf_op | source)
XLA Modules:
  0.0 86.5 jit_solution(12684133583065698752)
XLA Ops:
  0.6 83.7 %backward.1 = (bf16[16,64,128]{2,1,0:T(8,128)(2,1)}, bf16[64,32,128]{2,1,0:T(8,128)(2,1)}) custom-call(s32[3]{0:T(128)} %offs_hbm.1, bf16[16,64,128]{2,1,0:T(8,128)(2,1)} %bitcast.5, bf16[16,64,128]{2,1,0:T(8,128)(2,1)} %bitcast.6, bf16[1024,128]{1,0:T(8,128)(2,1)} %bitcast.7, bf16[1024,128]{1,0:T(8,128)(2,1)} %bitcast.8), custom_call_target="tpu_custom_call" | custom-call | flops 1610612736 | bytes 1835008 | tf_op jit(solution)/shard_map/backward/pallas_call | solution.py:241
  84.3 2.2 %by_token.1 = (bf16[16,64,128]{2,1,0:T(8,128)(2,1)}, bf16[16,64,128]{2,1,0:T(8,128)(2,1)}, bf16[16,64,128]{2,1,0:T(8,128)(2,1)}) custom-call(bf16[16,64,128]{2,1,0:T(8,128)(2,1)} %get-tuple-element.8.gq_in, bf16[64,32,128]{2,1,0:T(8,128)(2,1)} %get-tuple-element.9.kv_in), custom_call_target="tpu_custom_call" | custom-call | tf_op jit(solution)/shard_map/by_token/pallas_call | solution.py:287

commit v5 on v4

--- a/solution.py
+++ b/solution.py
@@ -117,6 +117,14 @@
     number = lane // toks
     shift = jnp.where(in_tok >= half, offs[2], offs[1]) - offs[0]
     local_pos = shift + in_tok % half
+
+    def return_queries(step, gq_t):
+        gq = jnp.transpose(gq_t * scale).astype(jnp.bfloat16)
+        send_q[step] = gq.reshape(GROUP, toks, hd)
+        exchange(
+            step, -1, lambda dev, i: send_q.at[step, i], lambda i: recv_q.at[me],
+            send_sem.at[1], recv_q_sem,
+        )
 
     for step in range(slots):
         pltpu.make_async_copy(recv_a.at[step], recv_a.at[step], recv_a_sem.at[step]).wait()
@@ -157,12 +165,8 @@
             gq_t = gq_t + jnp.dot(kt_ref[:, span], ds, preferred_element_type=jnp.float32)
             gk_acc[span, :] += jnp.dot(ds, q, preferred_element_type=jnp.float32)
             gv_acc[span, :] += jnp.dot(pb_ref[span, :], g, preferred_element_type=jnp.float32)
-        gq = jnp.transpose(gq_t * scale).astype(jnp.bfloat16)
-        send_q[step] = gq.reshape(GROUP, toks, hd)
-        exchange(
-            step, -1, lambda dev, i: send_q.at[step, i], lambda i: recv_q.at[me],
-            send_sem.at[1], recv_q_sem,
-        )
+        if step < slots - 1:
+            return_queries(step, gq_t)
 
     for i in range(slots):
         span = pl.ds(i * rows, rows)
@@ -178,6 +182,8 @@
             slot, 1, lambda dev, i: send_kv.at[dev], lambda i: recv_kv.at[me],
             send_sem.at[2], recv_kv_sem,
         )
+        if slot == 1:
+            return_queries(slots - 1, gq_t)
 
     stores = []
 

time: 86.7 us -> 87.3 us (level)
  no operation moved by 1% of the time
where the time goes in v5:
time: 87.3 us; the launch traced here: 87.1 us
  Pallas kernels  86.5 us (99%)
    pallas_call x1, Pallas kernels, body(): pl.pallas_call(kernel, out_shape=(out, jax.ShapeDtypeStruct((heads, 2 * t...  84.3 us
    pallas_call x1, Pallas kernels, body(): pl.pallas_call(by_token, out_shape=(out, out, out), in_specs=[hbm, hbm],...  2.15 us

profile of v5, /device:TPU:1, one launch (start us, length us, event | category | flops | bytes accessed | tf_op | source)
XLA Modules:
  0.0 87.1 jit_solution(12655674266386748561)
XLA Ops:
  0.6 84.3 %backward.1 = (bf16[16,64,128]{2,1,0:T(8,128)(2,1)}, bf16[64,32,128]{2,1,0:T(8,128)(2,1)}) custom-call(s32[3]{0:T(128)} %offs_hbm.1, bf16[16,64,128]{2,1,0:T(8,128)(2,1)} %bitcast.5, bf16[16,64,128]{2,1,0:T(8,128)(2,1)} %bitcast.6, bf16[1024,128]{1,0:T(8,128)(2,1)} %bitcast.7, bf16[1024,128]{1,0:T(8,128)(2,1)} %bitcast.8), custom_call_target="tpu_custom_call" | custom-call | flops 1610612736 | bytes 1835008 | tf_op jit(solution)/shard_map/backward/pallas_call | solution.py:247
  85.0 2.2 %by_token.1 = (bf16[16,64,128]{2,1,0:T(8,128)(2,1)}, bf16[16,64,128]{2,1,0:T(8,128)(2,1)}, bf16[16,64,128]{2,1,0:T(8,128)(2,1)}) custom-call(bf16[16,64,128]{2,1,0:T(8,128)(2,1)} %get-tuple-element.8.gq_in, bf16[64,32,128]{2,1,0:T(8,128)(2,1)} %get-tuple-element.9.kv_in), custom_call_target="tpu_custom_call" | custom-call | tf_op jit(solution)/shard_map/by_token/pallas_call | solution.py:293
